TPU v7x, 32 devices: a whole 2x2x4 slice. The times are simulated.
32 devices in a mesh: dp: 8 (over y, x, core), tensor: 4 (over z).
Axes of the slice: x: 2, y: 2, z: 4, core: 2. Of those that a mesh axis runs over, the one named last changes fastest.
Arguments:
- out_grad: bfloat16 [8, 256, 4096], P('dp', 'tensor'), may hold values from -6 to 6
- out_weight: bfloat16 [4096, 1024], P('dp', 'tensor'), may hold values from -0.1875 to 0.1875
- queries: bfloat16 [8, 256, 1024], P('dp', None, 'tensor'), may hold values from -5 to 5
- keys: bfloat16 [8, 256, 512], P('dp', None, 'tensor'), may hold values from -5 to 5, as said below
- values: bfloat16 [8, 256, 512], P('dp', None, 'tensor'), may hold values from -6 to 6, as said below
- segment_ids: int32 [8, 256], P('dp'), may hold values from 0 to 3, never falling along the last dimension, each value on 1 to 128 neighbouring positions
Outputs:
- d_queries: bfloat16 [8, 256, 1024], P('dp', None, 'tensor')
- d_keys: bfloat16 [8, 256, 512], P('dp', None, 'tensor')
- d_values: bfloat16 [8, 256, 512], P('dp', None, 'tensor')
- d_out_weight: float32 [4096, 1024], P('dp', 'tensor')
Inputs may be any that keep to these rules, and one draw needn't show every extreme that they name: `keys`: column blocks 2 g and 2 g + 1 are equal. `values`: column blocks 2 g and 2 g + 1 are equal.
All inputs are finite; a program needn't handle non-finite values.
Results may differ from a plain program's by a relative error of at most 0.018.
Values may be sent and summed in bfloat16 or wider, within the bound.
A program may use at most 128 MiB of HBM per device.

v0:
```python
import jax
import jax.numpy as jnp
from jax import lax
from jax.sharding import PartitionSpec as P

HD = 128


def from_partner(block, axis, bit):
    count = lax.axis_size(axis)
    route = []
    for low in range(count):
        high = low | 1 << bit
        if high != low and high < count:
            route += [(low, high), (high, low)]
    return lax.ppermute(block, axis, route)


def local(out_grad, out_weight, queries, keys, values, segment_ids):
    scale = HD ** (-0.5)
    grad_local = out_grad[0]
    query_rows = queries[0]
    length = query_rows.shape[0]
    width = query_rows.shape[1]
    heads_here = width // HD
    key_local = keys[0]
    value_local = values[0]
    query_heads = query_rows.reshape(length, heads_here, HD)
    scores = (
        jnp.einsum("qhd,kd->hqk", query_heads, key_local, preferred_element_type=jnp.float32)
        * scale
    )
    segments = segment_ids[0]
    position = jnp.arange(length)
    visible = (segments[:, None] == segments[None, :]) & (position[:, None] >= position[None, :])
    masked = jnp.where(visible[None], scores, -jnp.inf)
    top_score = jnp.max(masked, axis=-1, keepdims=True)
    raw_exp = jnp.exp(masked - top_score)
    attn_prob = raw_exp / jnp.sum(raw_exp, axis=-1, keepdims=True)
    prob_low = attn_prob.astype(jnp.bfloat16)
    attn_out = jnp.einsum(
        "hqk,kd->qhd", prob_low, value_local, preferred_element_type=jnp.float32
    ).astype(jnp.bfloat16)
    flat_out = attn_out.reshape(length, width)
    grad_full = lax.all_gather(grad_local, "tensor", axis=0, tiled=True)
    columns = grad_full
    grad_sum = jnp.dot(
        columns,
        lax.all_gather(out_weight, "dp", axis=0, tiled=True),
        preferred_element_type=jnp.float32,
    )
    columns = grad_full
    weight_rows = lax.psum_scatter(
        lax.dot_general(
            columns, flat_out, (((0,), (0,)), ((), ())), preferred_element_type=jnp.float32
        ).astype(jnp.bfloat16),
        "dp",
        scatter_dimension=0,
        tiled=True,
    ).astype(jnp.float32)
    grad_attn = grad_sum.astype(jnp.bfloat16)
    grad_heads = grad_attn.reshape(length, heads_here, HD)
    deltas = jnp.sum(grad_heads.astype(jnp.float32) * attn_out.astype(jnp.float32), axis=-1)
    grad_values = jnp.einsum(
        "hqk,qhd->kd", prob_low, grad_heads, preferred_element_type=jnp.float32
    )
    grad_prob = jnp.einsum(
        "qhd,kd->hqk", grad_heads, value_local, preferred_element_type=jnp.float32
    )
    grad_score = (attn_prob * (grad_prob - jnp.transpose(deltas)[:, :, None]) * scale).astype(
        jnp.bfloat16
    )
    grad_queries = jnp.einsum(
        "hqk,kd->qhd", grad_score, key_local, preferred_element_type=jnp.float32
    ).astype(jnp.bfloat16)
    grad_keys = jnp.einsum(
        "hqk,qhd->kd", grad_score, query_heads, preferred_element_type=jnp.float32
    )
    partner_keys, partner_values = (
        from_partner(grad_keys.astype(jnp.bfloat16), "tensor", 0).astype(grad_keys.dtype),
        from_partner(grad_values.astype(jnp.bfloat16), "tensor", 0).astype(grad_values.dtype),
    )
    keys_total = (grad_keys + partner_keys).astype(jnp.bfloat16)
    values_total = (grad_values + partner_values).astype(jnp.bfloat16)
    weight_grad = weight_rows / lax.axis_size("dp")
    return (
        grad_queries.reshape(1, length, width),
        keys_total[None],
        values_total[None],
        weight_grad,
    )


def solution(mesh):
    in_specs = (
        P("dp", "tensor", None),
        P("dp", "tensor"),
        P("dp", None, "tensor"),
        P("dp", None, "tensor"),
        P("dp", None, "tensor"),
        P("dp", None),
    )
    out_specs = (
        P("dp", None, "tensor"),
        P("dp", None, "tensor"),
        P("dp", None, "tensor"),
        P("dp", "tensor"),
    )
    return jax.shard_map(local, mesh=mesh, in_specs=in_specs, out_specs=out_specs, check_vma=False)
```

profile of v0, /device:TPU:0, one launch (start us, length us, event | category | flops | bytes accessed | tf_op | source)
XLA Modules:
  0.0 143.6 jit_solution(18421356278678418032)
XLA Ops:
  7.2 0.7 all-gather.6.cloned.1.call-update
  8.0 0.7 all-gather.4.cloned.1.call-update
  8.7 0.9 reshape_squeeze.3
  9.7 0.9 fusion.16
  10.5 0.3 fusion.55
  10.9 47.4 %all-gather.6.cloned.1.call-done = bf16[1,256,4096]{2,1,0:T(8,128)(2,1)} async-done(((bf16[1,64,4096]{2,1,0:T(8,128)(2,1)}), bf16[1,256,4096]{2,1,0:T(8,128)(2,1)}) %all-gather.6.cloned.1.call-update) | async-done | bytes 2097168 | tf_op jit(solution)/shard_map/all_gather | solution.py:45
  58.3 28.5 %all-gather.4.cloned.1.call-done = bf16[4096,256]{1,0:T(8,128)(2,1)} async-done(((bf16[512,256]{1,0:T(8,128)(2,1)}), bf16[4096,256]{1,0:T(8,128)(2,1)}) %all-gather.4.cloned.1.call-update) | async-done | bytes 2097168 | tf_op jit(solution)/shard_map/all_gather | solution.py:49
  86.8 3.1 %fusion.13 = bf16[256,256]{0,1:T(8,128)(2,1)S(1)} fusion(bf16[4096,256]{1,0:T(8,128)(2,1)} %all-gather.4.cloned.1.call-done, bf16[1,256,4096]{2,1,0:T(8,128)(2,1)} %all-gather.6.cloned.1.call-done), kind=kOutput, calls=%fused_computation.18 | convolution fusion | flops 536936448 | bytes 4325376 | tf_op jit(solution)/shard_map/dot_general | solution.py:47
  90.0 0.5 multiply_reduce_fusion
  90.5 1.0 copy-done.1
  91.5 2.1 %fusion.1 = bf16[4096,256]{0,1:T(8,128)(2,1)} fusion(bf16[256,256]{0,1:T(8,128)(2,1)S(1)} %bitcast.105, bf16[1,256,4096]{2,1,0:T(8,128)(2,1)S(1)} %copy-done.1), kind=kOutput, calls=%fused_computation.2 | convolution fusion | flops 537919488 | bytes 4325376 | tf_op jit(solution)/shard_map/dot_general | solution.py:54
  93.8 0.2 fusion.64
  94.1 1.5 %collective-permute-start = (bf16[256,128]{1,0:T(8,128)(2,1)S(1)}, bf16[256,128]{1,0:T(8,128)(2,1)S(1)}, u32[]{:S(2)}, u32[]{:S(2)}) collective-permute-start(bf16[256,128]{1,0:T(8,128)(2,1)S(1)} %get-tuple-element.12), channel_id=1, source_target_pairs={{0,1},{1,0},{2,3},{3,2},{4,5},{5,4},{6,7},{7,6},{8,9},{9,8},{10,11... | collective-permute-start | bytes 196616 | tf_op jit(solution)/shard_map/ppermute | solution.py:16
  95.6 0.2 convolution_convert_fusion.1
  95.8 0.5 fusion.65
  96.4 0.8 copy.19
  97.1 0.5 collective-permute-start.1
  97.7 0.7 collective-permute-done
  98.4 0.6 fusion.20
  99.0 2.3 %collective-permute-done.1 = bf16[256,128]{1,0:T(8,128)(2,1)S(1)} collective-permute-done((bf16[256,128]{1,0:T(8,128)(2,1)S(1)}, bf16[256,128]{1,0:T(8,128)(2,1)S(1)}, u32[]{:S(2)}, u32[]{:S(2)}) %collective-permute-start.1) | collective-permute-done | bytes 65568 | tf_op jit(solution)/shard_map/ppermute | solution.py:16
  101.4 0.6 fusion.21
  102.0 33.0 %reduce-scatter.2.cloned.1.call-done = bf16[512,256]{0,1:T(8,128)(2,1)} async-done(((bf16[4096,256]{0,1:T(8,128)(2,1)}), bf16[512,256]{0,1:T(8,128)(2,1)}) %reduce-scatter.2.cloned.1.call-update) | async-done | bytes 262160 | tf_op jit(solution)/shard_map/reduce_scatter | solution.py:53
  135.0 1.0 convert_multiply_fusion
  136.0 1.0 copy.20
  (10 shorter events, 0.4 us)
Async XLA Ops:
  7.2 3.4 %copy-start = (bf16[1,256,128]{2,1,0:T(8,128)(2,1)S(1)}, bf16[1,256,128]{2,1,0:T(8,128)(2,1)}, u32[]{:S(2)}) copy-start(bf16[1,256,128]{2,1,0:T(8,128)(2,1)} %param.9) | copy-start | bytes 196612
  7.2 51.1 %all-gather.6.cloned.1.call-start = ((), (), s32[]{:S(2)}) async-start(), calls=%async_computation.3 | async-start | bytes 2621440 | tf_op jit(solution)/shard_map/all_gather | solution.py:45
  7.9 78.9 %all-gather.4.cloned.1.call-start = ((), (), s32[]{:S(2)}) async-start(), calls=%async_computation.1 | async-start | bytes 2359296 | tf_op jit(solution)/shard_map/all_gather | solution.py:49
  8.7 126.3 %reduce-scatter.2.cloned.1.call-start = ((), (), s32[]{:S(2)}) async-start(), calls=%async_computation.2 | async-start | bytes 2359296 | tf_op jit(solution)/shard_map/reduce_scatter | solution.py:53
  10.9 79.1 %copy-start.2 = (bf16[1,256,128]{2,1,0:T(8,128)(2,1)S(1)}, bf16[1,256,128]{2,1,0:T(8,128)(2,1)}, u32[]{:S(2)}) copy-start(bf16[1,256,128]{2,1,0:T(8,128)(2,1)} %param.10) | copy-start | bytes 196612
  89.9 1.6 %copy-start.1 = (bf16[1,256,4096]{2,1,0:T(8,128)(2,1)S(1)}, bf16[1,256,4096]{2,1,0:T(8,128)(2,1)}, u32[]{:S(2)}) copy-start(bf16[1,256,4096]{2,1,0:T(8,128)(2,1)} %all-gather.6.cloned.1.call-done) | copy-start | bytes 6291460
  94.1 4.3 %collective-permute-start = (bf16[256,128]{1,0:T(8,128)(2,1)S(1)}, bf16[256,128]{1,0:T(8,128)(2,1)S(1)}, u32[]{:S(2)}, u32[]{:S(2)}) collective-permute-start(bf16[256,128]{1,0:T(8,128)(2,1)S(1)} %get-tuple-element.12), channel_id=1, source_target_pairs={{0,1},{1,0},{2,3},{3,2},{4,5},{5,4},{6,7},{7,6},{8,9},{9,8},{10,11... | collective-permute-start | bytes 196616 | tf_op jit(solution)/shard_map/ppermute | solution.py:16
  97.1 4.3 %collective-permute-start.1 = (bf16[256,128]{1,0:T(8,128)(2,1)S(1)}, bf16[256,128]{1,0:T(8,128)(2,1)S(1)}, u32[]{:S(2)}, u32[]{:S(2)}) collective-permute-start(bf16[256,128]{1,0:T(8,128)(2,1)S(1)} %get-tuple-element.14), channel_id=1, source_target_pairs={{0,1},{1,0},{2,3},{3,2},{4,5},{5,4},{6,7},{7,6},{8,9},{9,8},{10,11... | collective-permute-start | bytes 196616 | tf_op jit(solution)/shard_map/ppermute | solution.py:16
Sparse Core Ops, SparseCore 0:
  9.6 48.6 all-gather.5
  60.1 26.5 all-gather.3
  93.7 41.2 reduce-scatter.1
where the time goes:
time: 144 us
  waiting for transfers between devices  113 us (78%)
  between operations  13.8 us (10%)
  matrix products  7.24 us (5%)
  local copies, waits for them, and re-layouts  3.77 us (3%)
  other arithmetic  3.15 us (2%)
  starting transfers between devices  2.2 us (2%)
    all_gather x1, waiting for transfers between devices, local(): grad_full = lax.all_gather(grad_local, 'tensor', axis=0, tiled=True)  47.4 us
    reduce_scatter x1, waiting for transfers between devices, local(): lax.psum_scatter(lax.dot_general(columns, flat_out, (((0,), (0,)), ((), (...  33 us
    all_gather x1, waiting for transfers between devices, local(): lax.all_gather(out_weight, 'dp', axis=0, tiled=True)  28.5 us
    dot_general x1, matrix products, local(): jnp.dot(columns, lax.all_gather(out_weight, 'dp', axis=0, tiled=True), pr...  3.15 us
    ppermute x2, waiting for transfers between devices, from_partner(): return lax.ppermute(block, axis, route)  3.08 us
  transfers between devices with their start and end apart: 5, of which 5 were waited for; matrix products, arithmetic and copies ran while one was open for 4% of the time, Pallas kernels for 0%

commit v1 on v0

--- a/solution.py
+++ b/solution.py
@@ -4,6 +4,14 @@
 from jax.sharding import PartitionSpec as P
 
 HD = 128
+
+
+def compute_outputs(field, axis_no):
+    field = jnp.moveaxis(field, 0, axis_no)
+    formed = field.shape
+    return field.reshape(
+        *formed[:axis_no], formed[axis_no] * formed[axis_no + 1], *formed[axis_no + 2 :]
+    )
 
 
 def from_partner(block, axis, bit):
@@ -42,7 +50,15 @@
         "hqk,kd->qhd", prob_low, value_local, preferred_element_type=jnp.float32
     ).astype(jnp.bfloat16)
     flat_out = attn_out.reshape(length, width)
-    grad_full = lax.all_gather(grad_local, "tensor", axis=0, tiled=True)
+    workers = lax.axis_size("tensor")
+    column = tuple(((j, (j + 1) % workers) for j in range(workers)))
+    ledger = [grad_local]
+    while len(ledger) < workers:
+        small = lax.ppermute(ledger[-1], perm=column, axis_name="tensor")
+        ledger.append(small)
+    w_next = lax.axis_index("tensor")
+    ledger = jnp.stack(ledger)[(w_next - jnp.arange(workers)) % workers]
+    grad_full = compute_outputs(ledger, 0)
     columns = grad_full
     grad_sum = jnp.dot(
         columns,

time: 144 us -> 111 us (0.77)
  waiting for transfers between devices: 113 us -> 75.3 us
  starting transfers between devices: 2.2 us -> 5.24 us
  other arithmetic: 3.15 us -> 5.51 us
    all_gather x1 -> x0, waiting for transfers between devices: 47.4 us -> none  [local(): grad_full = lax.all_gather(grad_local, 'tensor', axis=0, tiled=True)]
    ppermute x0 -> x3, waiting for transfers between devices: none -> 40.9 us  [local(): small = lax.ppermute(ledger[-1], perm=column, axis_name='tensor')]
    all_gather x1, waiting for transfers between devices: 28.5 us -> 0.02 us  [local(): lax.all_gather(out_weight, 'dp', axis=0, tiled=True)]
    ppermute x0 -> x3, starting transfers between devices: none -> 3.08 us  [local(): small = lax.ppermute(ledger[-1], perm=column, axis_name='tensor')]
    gather x0 -> x1, local copies, waits for them, and re-layouts: none -> 2.27 us  [local(): ledger = jnp.stack(ledger)[(w_next - jnp.arange(workers)) % workers]]
    unnamed x8 -> x7, local copies, waits for them, and re-layouts: 2.83 us -> 0.78 us
    another operation x0 -> x1, other arithmetic: none -> 1.57 us  [local(): ledger = jnp.stack(ledger)[(w_next - jnp.arange(workers)) % workers]]
  transfers between devices with their start and end apart: 5 -> 7, of which waited for: 5 -> 6; matrix products, arithmetic and copies ran while one was open for 4% -> 8% of each run, Pallas kernels for 0% -> 0%
where the time goes in v1:
time: 111 us
  waiting for transfers between devices  75.3 us (68%)
  between operations  14.2 us (13%)
  matrix products  6.69 us (6%)
  other arithmetic  5.51 us (5%)
  starting transfers between devices  5.24 us (5%)
  local copies, waits for them, and re-layouts  3.99 us (4%)
    ppermute x3, waiting for transfers between devices, local(): small = lax.ppermute(ledger[-1], perm=column, axis_name='tensor')  40.9 us
    reduce_scatter x1, waiting for transfers between devices, local(): lax.psum_scatter(lax.dot_general(columns, flat_out, (((0,), (0,)), ((), (...  32.1 us
    ppermute x3, starting transfers between devices, local(): small = lax.ppermute(ledger[-1], perm=column, axis_name='tensor')  3.08 us
    dot_general x1, matrix products, local(): jnp.dot(columns, lax.all_gather(out_weight, 'dp', axis=0, tiled=True), pr...  2.55 us
    gather x1, local copies, waits for them, and re-layouts, local(): ledger = jnp.stack(ledger)[(w_next - jnp.arange(workers)) % workers]  2.27 us
  transfers between devices with their start and end apart: 7, of which 6 were waited for; matrix products, arithmetic and copies ran while one was open for 8% of the time, Pallas kernels for 0%

profile of v1, /device:TPU:0, one launch (start us, length us, event | category | flops | bytes accessed | tf_op | source)
XLA Modules:
  0.0 110.9 jit_solution(935879947387347828)
XLA Ops:
  7.2 0.7 all-gather.2.cloned.1.call-update
  8.0 3.1 %collective-permute-start = (bf16[64,4096]{1,0:T(8,128)(2,1)}, bf16[64,4096]{1,0:T(8,128)(2,1)S(1)}, u32[]{:S(2)}, u32[]{:S(2)}) collective-permute-start(bf16[64,4096]{1,0:T(8,128)(2,1)} %bitcast.105), channel_id=1, source_target_pairs={{0,1},{1,2},{2,3},{3,0},{4,5},{5,6},{6,7},{7,4},{8,9},{9,10},{10,1... | collective-permute-start | bytes 1572872 | tf_op jit(solution)/shard_map/ppermute | solution.py:57
  11.0 14.2 %collective-permute-done = bf16[64,4096]{1,0:T(8,128)(2,1)S(1)} collective-permute-done((bf16[64,4096]{1,0:T(8,128)(2,1)}, bf16[64,4096]{1,0:T(8,128)(2,1)S(1)}, u32[]{:S(2)}, u32[]{:S(2)}) %collective-permute-start) | collective-permute-done | bytes 524320 | tf_op jit(solution)/shard_map/ppermute | solution.py:57
  25.2 14.9 %collective-permute-done.1 = bf16[64,4096]{1,0:T(8,128)(2,1)S(1)} collective-permute-done((bf16[64,4096]{1,0:T(8,128)(2,1)S(1)}, bf16[64,4096]{1,0:T(8,128)(2,1)S(1)}, u32[]{:S(2)}, u32[]{:S(2)}) %collective-permute-start.1) | collective-permute-done | bytes 524320 | tf_op jit(solution)/shard_map/ppermute | solution.py:57
  40.1 0.9 reshape_squeeze.3
  41.1 0.9 fusion.9
  41.9 0.3 fusion.50
  42.3 11.8 %collective-permute-done.2 = bf16[64,4096]{1,0:T(8,128)(2,1)S(1)} collective-permute-done((bf16[64,4096]{1,0:T(8,128)(2,1)S(1)}, bf16[64,4096]{1,0:T(8,128)(2,1)S(1)}, u32[]{:S(2)}, u32[]{:S(2)}) %collective-permute-start.2) | collective-permute-done | bytes 524320 | tf_op jit(solution)/shard_map/ppermute | solution.py:57
  54.1 1.6 %pad_maximum_fusion = bf16[4,64,4096]{2,1,0:T(8,128)(2,1)} fusion(bf16[1,64,4096]{2,1,0:T(8,128)(2,1)S(1)} %bitcast.108, bf16[1,64,4096]{2,1,0:T(8,128)(2,1)S(1)} %bitcast.107, bf16[1,64,4096]{2,1,0:T(8,128)(2,1)S(1)} %bitcast.106, bf16[1,64,4096]{2,1,0:T(8,128)(2,1)S(1)} %copy-done.1), kind=kLoop, calls=%fused_computation.3 | loop fusion | flops 3145728 | bytes 4194304 | tf_op jit(solution)/shard_map/stack | solution.py:60
  55.7 2.3 %gather_fusion = bf16[4,64,4096]{2,1,0:T(8,128)(2,1)S(1)} fusion(bf16[4,64,4096]{2,1,0:T(8,128)(2,1)} %pad_maximum_fusion, s32[1024]{0:T(1024)S(1)} %pad_clamp_fusion), kind=kCustom, calls=%fused_computation | custom fusion | bytes 4194320 | tf_op jit(solution)/shard_map/gather | solution.py:60
  58.0 2.5 %convolution_convert_fusion.3 = bf16[256,256]{0,1:T(8,128)(2,1)S(1)} fusion(bf16[256,4096]{1,0:T(8,128)(2,1)S(1)} %bitcast.102, bf16[4096,256]{1,0:T(8,128)(2,1)} %all-gather.2.cloned.1.call-done), kind=kOutput, calls=%fused_computation.16 | convolution fusion | flops 536936448 | bytes 4325376 | tf_op jit(solution)/shard_map/dot_general | solution.py:63
  60.6 0.5 multiply_reduce_fusion
  61.1 2.1 %convolution_convert_fusion = bf16[4096,256]{1,0:T(8,128)(2,1)} fusion(bf16[256,4096]{1,0:T(8,128)(2,1)S(1)} %bitcast.103, bf16[256,256]{0,1:T(8,128)(2,1)S(1)} %bitcast.109), kind=kOutput, calls=%fused_computation.2 | convolution fusion | flops 537919488 | bytes 4325376 | tf_op jit(solution)/shard_map/dot_general | solution.py:70
  63.4 0.2 fusion.59
  63.7 0.2 convolution_convert_fusion.1
  64.0 0.5 fusion.60
  64.5 0.8 copy.19
  65.3 2.0 %collective-permute-start.4 = (bf16[256,128]{1,0:T(8,128)(2,1)S(1)}, bf16[256,128]{1,0:T(8,128)(2,1)S(1)}, u32[]{:S(2)}, u32[]{:S(2)}) collective-permute-start(bf16[256,128]{1,0:T(8,128)(2,1)S(1)} %get-tuple-element.14), channel_id=1, source_target_pairs={{0,1},{1,0},{2,3},{3,2},{4,5},{5,4},{6,7},{7,6},{8,9},{9,8},{10,11... | collective-permute-start | bytes 196616 | tf_op jit(solution)/shard_map/ppermute | solution.py:24
  67.3 0.7 collective-permute-done.3
  68.0 0.6 fusion.13
  68.6 0.9 collective-permute-done.4
  69.6 0.6 fusion.14
  70.2 32.1 %reduce-scatter.2.cloned.1.call-done = bf16[512,256]{1,0:T(8,128)(2,1)} async-done(((bf16[4096,256]{1,0:T(8,128)(2,1)}), bf16[512,256]{1,0:T(8,128)(2,1)}) %reduce-scatter.2.cloned.1.call-update) | async-done | bytes 262160 | tf_op jit(solution)/shard_map/reduce_scatter | solution.py:69
  102.3 1.8 %convert_multiply_fusion = f32[512,256]{1,0:T(8,128)} fusion(bf16[512,256]{1,0:T(8,128)(2,1)} %reduce-scatter.2.cloned.1.call-done), kind=kLoop, calls=%fused_computation.19 | loop fusion | flops 262144 | bytes 786432 | tf_op jit(solution)/shard_map/div | solution.py:101
  (16 shorter events, 0.4 us)
Async XLA Ops:
  7.2 34.8 %copy-start = (bf16[1,256,128]{2,1,0:T(8,128)(2,1)S(1)}, bf16[1,256,128]{2,1,0:T(8,128)(2,1)}, u32[]{:S(2)}) copy-start(bf16[1,256,128]{2,1,0:T(8,128)(2,1)} %param.9) | copy-start | bytes 196612
  7.2 46.9 %copy-start.1 = (bf16[1,64,4096]{2,1,0:T(8,128)(2,1)S(1)}, bf16[1,64,4096]{2,1,0:T(8,128)(2,1)}, u32[]{:S(2)}) copy-start(bf16[1,64,4096]{2,1,0:T(8,128)(2,1)} %param.6) | copy-start | bytes 1572868
  7.2 50.8 %all-gather.2.cloned.1.call-start = ((), (), s32[]{:S(2)}) async-start(), calls=%async_computation.1 | async-start | bytes 2359296 | tf_op jit(solution)/shard_map/all_gather | solution.py:65
  7.9 94.4 %reduce-scatter.2.cloned.1.call-start = ((), (), s32[]{:S(2)}) async-start(), calls=%async_computation.2 | async-start | bytes 2359296 | tf_op jit(solution)/shard_map/reduce_scatter | solution.py:69
  8.0 17.2 %collective-permute-start = (bf16[64,4096]{1,0:T(8,128)(2,1)}, bf16[64,4096]{1,0:T(8,128)(2,1)S(1)}, u32[]{:S(2)}, u32[]{:S(2)}) collective-permute-start(bf16[64,4096]{1,0:T(8,128)(2,1)} %bitcast.105), channel_id=1, source_target_pairs={{0,1},{1,2},{2,3},{3,0},{4,5},{5,6},{6,7},{7,4},{8,9},{9,10},{10,1... | collective-permute-start | bytes 1572872 | tf_op jit(solution)/shard_map/ppermute | solution.py:57
  25.2 14.9 %collective-permute-start.1 = (bf16[64,4096]{1,0:T(8,128)(2,1)S(1)}, bf16[64,4096]{1,0:T(8,128)(2,1)S(1)}, u32[]{:S(2)}, u32[]{:S(2)}) collective-permute-start(bf16[64,4096]{1,0:T(8,128)(2,1)S(1)} %collective-permute-done), channel_id=1, source_target_pairs={{0,1},{1,2},{2,3},{3,0},{4,5},{5,6},{6,7},{7,4},{8,9},{9,10},{10,1... | collective-permute-start | bytes 1572872 | tf_op jit(solution)/shard_map/ppermute | solution.py:57
  40.1 14.0 %collective-permute-start.2 = (bf16[64,4096]{1,0:T(8,128)(2,1)S(1)}, bf16[64,4096]{1,0:T(8,128)(2,1)S(1)}, u32[]{:S(2)}, u32[]{:S(2)}) collective-permute-start(bf16[64,4096]{1,0:T(8,128)(2,1)S(1)} %collective-permute-done.1), channel_id=1, source_target_pairs={{0,1},{1,2},{2,3},{3,0},{4,5},{5,6},{6,7},{7,4},{8,9},{9,10},{10,1... | collective-permute-start | bytes 1572872 | tf_op jit(solution)/shard_map/ppermute | solution.py:57
  58.0 2.6 %copy-start.2 = (bf16[1,256,128]{2,1,0:T(8,128)(2,1)S(1)}, bf16[1,256,128]{2,1,0:T(8,128)(2,1)}, u32[]{:S(2)}) copy-start(bf16[1,256,128]{2,1,0:T(8,128)(2,1)} %param.10) | copy-start | bytes 196612
  63.7 4.3 %collective-permute-start.3 = (bf16[256,128]{1,0:T(8,128)(2,1)S(1)}, bf16[256,128]{1,0:T(8,128)(2,1)S(1)}, u32[]{:S(2)}, u32[]{:S(2)}) collective-permute-start(bf16[256,128]{1,0:T(8,128)(2,1)S(1)} %get-tuple-element.12), channel_id=1, source_target_pairs={{0,1},{1,0},{2,3},{3,2},{4,5},{5,4},{6,7},{7,6},{8,9},{9,8},{10,11... | collective-permute-start | bytes 196616 | tf_op jit(solution)/shard_map/ppermute | solution.py:24
  65.3 4.3 %collective-permute-start.4 = (bf16[256,128]{1,0:T(8,128)(2,1)S(1)}, bf16[256,128]{1,0:T(8,128)(2,1)S(1)}, u32[]{:S(2)}, u32[]{:S(2)}) collective-permute-start(bf16[256,128]{1,0:T(8,128)(2,1)S(1)} %get-tuple-element.14), channel_id=1, source_target_pairs={{0,1},{1,0},{2,3},{3,2},{4,5},{5,4},{6,7},{7,6},{8,9},{9,8},{10,11... | collective-permute-start | bytes 196616 | tf_op jit(solution)/shard_map/ppermute | solution.py:24
Sparse Core Ops, SparseCore 0:
  9.9 30.5 all-gather.1
  63.3 38.9 reduce-scatter.1
